TPU v7x, 128 devices: a whole 4x4x4 slice. The times are simulated.
128 devices in a mesh: expert: 8 (over z, core), shard: 16 (over y, x).
Axes of the slice: x: 4, y: 4, z: 4, core: 2. Of those that a mesh axis runs over, the one named last changes fastest.
Arguments:
- tokens: bfloat16 [1024, 6144], P('expert'), may hold values from -6 to 6
- routes: int32 [1024, 2], P('expert'), may hold values from 0 to 7, all different within a row; in each aligned block of 128 rows (0 to 127, 128 to 255, ...) at most 64 rows name the same one
- route_weights: float32 [1024, 2], P('expert'), may hold values from 0.1 to 1
- out_grad: bfloat16 [1024, 6144], P('expert'), may hold values from -6 to 6
- w_gate: bfloat16 [8, 6144, 8192], P('expert', None, 'shard'), may hold values from -0.078125 to 0.078125
- w_up: bfloat16 [8, 6144, 8192], P('expert', None, 'shard'), may hold values from -0.078125 to 0.078125
- w_down: bfloat16 [8, 8192, 6144], P('expert', 'shard'), may hold values from -0.0625 to 0.0625
Outputs:
- moe_out: bfloat16 [1024, 6144], P('expert')
- input_grad: bfloat16 [1024, 6144], P('expert')
Inputs may be any that keep to these rules, and one draw needn't show every extreme that they name: `routes`: the two experts of a token differ. In each aligned block of 128 rows (the tokens of one expert group) no expert is named by more than 64 rows, and in every draw some expert is named by exactly 64 rows of some block.
All inputs are finite; a program needn't handle non-finite values.
Results may differ from a plain program's by a relative error of at most 0.02.
Values may be sent and summed in bfloat16 or wider, within the bound.
No kernel may reach another device: no remote copies, remote signals or barrier semaphores. Data moves between devices by JAX's collectives and lax.ppermute only.
A program may use at most 128 MiB of HBM per device.

v0:
```python
import jax
import jax.numpy as jnp
from jax import lax
from jax.sharding import PartitionSpec as P


def backward_terms(rows_g, gate_act, up_act, w_gate, w_up, w_down):
    contract = (((1,), (1,)), ((), ()))
    d_hidden = lax.dot_general(rows_g, w_down[0], contract, preferred_element_type=jnp.float32)
    sigmoid_g = jax.nn.sigmoid(gate_act)
    d_gate = (d_hidden * up_act * sigmoid_g * (1.0 + gate_act * (1.0 - sigmoid_g))).astype(
        jnp.bfloat16
    )
    d_up = (d_hidden * gate_act * sigmoid_g).astype(jnp.bfloat16)
    grad_part = lax.dot_general(d_gate, w_gate[0], contract, preferred_element_type=jnp.float32)
    return grad_part + lax.dot_general(d_up, w_up[0], contract, preferred_element_type=jnp.float32)


def weighted_pair(returned, target, route_weights, count_rows, model_width):
    flat_rows = returned.reshape(-1, model_width)
    chosen = flat_rows[target].reshape(count_rows, 2, model_width).astype(jnp.float32)
    total = route_weights[:, 0:1] * chosen[:, 0, :] + route_weights[:, 1:2] * chosen[:, 1, :]
    return total.astype(jnp.bfloat16)


def per_device(tokens, routes, route_weights, out_grad, w_gate, w_up, w_down):
    count_rows, model_width = tokens.shape
    groups = lax.axis_size("expert")
    per_expert = 4 * count_rows // groups
    slot_count = groups * per_expert
    picked = (routes[:, :, None] == jnp.arange(groups, dtype=jnp.int32)[None, None, :]).astype(
        jnp.int32
    )
    picked = picked.reshape(2 * count_rows, groups)
    before = jnp.sum((jnp.cumsum(picked, axis=0) - picked) * picked, axis=1)
    target = routes.reshape(-1) * per_expert + before
    matches = target[None, :] == jnp.arange(slot_count, dtype=jnp.int32)[:, None]
    placed = matches.reshape(slot_count, count_rows, 2)
    dispatch = jnp.any(placed, axis=2).astype(jnp.bfloat16)
    send_rows = (
        jnp.dot(dispatch, tokens, preferred_element_type=jnp.float32)
        .astype(jnp.bfloat16)
        .reshape(groups, per_expert, model_width)
    )
    send_grad = (
        jnp.dot(dispatch, out_grad, preferred_element_type=jnp.float32)
        .astype(jnp.bfloat16)
        .reshape(groups, per_expert, model_width)
    )
    rows_x, rows_g = (
        lax.all_to_all(send_rows, "expert", split_axis=0, concat_axis=0, tiled=True),
        lax.all_to_all(send_grad, "expert", split_axis=0, concat_axis=0, tiled=True),
    )
    rows_x = rows_x.reshape(slot_count, model_width)
    rows_g = rows_g.reshape(slot_count, model_width)
    gate_act = jnp.dot(rows_x, w_gate[0], preferred_element_type=jnp.float32)
    up_act = jnp.dot(rows_x, w_up[0], preferred_element_type=jnp.float32)
    hidden = (jax.nn.silu(gate_act) * up_act).astype(jnp.bfloat16)
    out_part = jnp.dot(hidden, w_down[0], preferred_element_type=jnp.float32).reshape(
        groups, per_expert, model_width
    )
    out_sum = lax.psum_scatter(
        out_part.astype(jnp.bfloat16), "shard", scatter_dimension=1, tiled=True
    )
    out_home = lax.all_to_all(out_sum, "expert", split_axis=0, concat_axis=0, tiled=True)
    out_back = lax.all_gather(out_home, "shard", axis=1, tiled=True)
    grad_part = backward_terms(rows_g, gate_act, up_act, w_gate, w_up, w_down).reshape(
        groups, per_expert, model_width
    )
    grad_sum = lax.psum_scatter(
        grad_part.astype(jnp.bfloat16), "shard", scatter_dimension=1, tiled=True
    )
    grad_home = lax.all_to_all(grad_sum, "expert", split_axis=0, concat_axis=0, tiled=True)
    grad_back = lax.all_gather(grad_home, "shard", axis=1, tiled=True)
    moe_out = weighted_pair(out_back, target, route_weights, count_rows, model_width)
    input_grad = weighted_pair(grad_back, target, route_weights, count_rows, model_width)
    return (moe_out, input_grad)


def solution(mesh):
    in_specs = (
        P("expert", None),
        P("expert", None),
        P("expert", None),
        P("expert", None),
        P("expert", None, "shard"),
        P("expert", None, "shard"),
        P("expert", "shard", None),
    )
    out_specs = (P("expert", None), P("expert", None))
    return jax.shard_map(
        per_device, mesh=mesh, in_specs=in_specs, out_specs=out_specs, check_vma=False
    )
```

profile of v0, /device:TPU:1, one launch (start us, length us, event | category | flops | bytes accessed | tf_op | source)
XLA Modules:
  0.0 559.2 jit_solution(7522904941379312739)
XLA Ops:
  7.2 0.0 copy-start
  7.2 0.9 copy.47
  8.1 0.1 eq.44
  8.2 0.1 eq.40
  8.4 0.6 reduce-window.6
  9.0 0.2 slice_reduce_fusion
  9.2 0.1 fusion.22
  9.3 0.1 reduce_sum.14
  9.5 0.1 copy.50
  9.5 0.1 fusion.20
  9.6 0.0 copy-done
  9.6 4.4 convolution_convert_fusion.2
  14.0 0.0 copy-start.2
  14.0 6.9 %all-to-all-start = ((bf16[8,64,6144]{2,1,0:T(8,128)(2,1)}), bf16[8,64,6144]{2,1,0:T(8,128)(2,1)}, u32[]{:S(2)}, u32[]{:S(2)}) async-start(bf16[8,64,6144]{2,1,0:T(8,128)(2,1)} %bitcast.79), calls=%async_computation | async-start | bytes 12582912 | tf_op jit(solution)/shard_map/all_to_all | solution.py:51
  21.0 0.0 copy-done.2
  21.0 4.4 convolution_convert_fusion
  25.4 67.0 %all-to-all-done = bf16[8,64,6144]{2,1,0:T(8,128)(2,1)} async-done(((bf16[8,64,6144]{2,1,0:T(8,128)(2,1)}), bf16[8,64,6144]{2,1,0:T(8,128)(2,1)}, u32[]{:S(2)}, u32[]{:S(2)}) %all-to-all-start) | async-done | bytes 6291488 | tf_op jit(solution)/shard_map/all_to_all | solution.py:51
  92.3 5.5 all-to-all-start.2
  97.9 0.0 reduce-scatter.5.cloned.1.call-start
  97.9 7.5 %fusion.8 = f32[512,512]{1,0:T(8,128)S(1)} fusion(bf16[512,6144]{1,0:T(8,128)(2,1)} %bitcast.4, bf16[1,6144,512]{2,1,0:T(8,128)(2,1)} %param.11), kind=kOutput, calls=%fused_computation.14 | convolution fusion | flops 3221225472 | bytes 13631488 | tf_op jit(solution)/shard_map/dot_general | solution.py:56
  105.4 8.2 %multiply_convert_fusion.2 = (bf16[512,512]{1,0:T(8,128)(2,1)S(1)}, f32[512,512]{1,0:T(8,128)S(1)}) fusion(f32[512,512]{1,0:T(8,128)S(1)} %fusion.8, bf16[512,6144]{1,0:T(8,128)(2,1)} %bitcast.4, bf16[1,6144,512]{2,1,0:T(8,128)(2,1)} %param.12), kind=kOutput, calls=%fused_computation.30 | convolution fusion | flops 3222798336 | bytes 15204352 | tf_op jit(solution)/shard_map/dot_general | solution.py:57
  113.5 55.8 %all-to-all-done.2 = bf16[8,64,6144]{2,1,0:T(8,128)(2,1)} async-done(((bf16[8,64,6144]{2,1,0:T(8,128)(2,1)}), bf16[8,64,6144]{2,1,0:T(8,128)(2,1)}, u32[]{:S(2)}, u32[]{:S(2)}) %all-to-all-start.2) | async-done | bytes 6291488 | tf_op jit(solution)/shard_map/all_to_all | solution.py:52
  169.3 7.5 %fusion.1 = f32[512,512]{1,0:T(8,128)S(1)} fusion(bf16[512,6144]{1,0:T(8,128)(2,1)} %bitcast.17, bf16[1,512,6144]{2,1,0:T(8,128)(2,1)} %param.13), kind=kOutput, calls=%fused_computation.7 | convolution fusion | flops 3221225472 | bytes 13631488 | tf_op jit(solution)/shard_map/dot_general | solution.py:9
  176.8 0.0 copy-start.3
  176.8 1.0 copy-done.3
  177.8 9.4 %fusion.6 = f32[512,6144]{1,0:T(8,128)} fusion(bf16[1,6144,512]{2,1,0:T(8,128)(2,1)} %param.11, f32[512,512]{1,0:T(8,128)S(1)} %fusion.8, f32[512,512]{1,0:T(8,128)S(1)} %fusion.1, f32[512,512]{1,0:T(8,128)S(1)} %get-tuple-element.13), kind=kOutput, calls=%fused_computation.12 | convolution fusion | flops 3223846912 | bytes 22020096 | tf_op jit(solution)/shard_map/dot_general | solution.py:15
  187.2 12.8 %add_convert_fusion = bf16[512,6144]{1,0:T(8,128)(2,1)} fusion(f32[512,6144]{1,0:T(8,128)} %fusion.6, bf16[1,6144,512]{2,1,0:T(8,128)(2,1)} %param.12, f32[512,512]{1,0:T(8,128)} %copy-done.3, f32[512,512]{1,0:T(8,128)S(1)} %fusion.8), kind=kOutput, calls=%fused_computation.2 | convolution fusion | flops 3229089792 | bytes 27262976 | tf_op jit(solution)/shard_map/dot_general | solution.py:16
  199.9 8.9 %copy.57 = bf16[8,64,6144]{2,0,1:T(8,128)(2,1)} copy(bf16[8,64,6144]{2,1,0:T(8,128)(2,1)} %bitcast.80) | data formatting | bytes 12582912 | tf_op jit(solution)/shard_map/convert_element_type | solution.py:71
  208.8 0.0 reduce-scatter.5.cloned.1.call-update
  208.8 0.0 reduce-scatter.3.cloned.1.call-start
  208.9 6.4 %convolution_convert_fusion.1 = bf16[8,64,6144]{2,1,0:T(8,128)(2,1)S(1)} fusion(bf16[8,64,512]{2,1,0:T(8,128)(2,1)S(1)} %bitcast.83, bf16[1,512,6144]{2,1,0:T(8,128)(2,1)} %param.13), kind=kOutput, calls=%fused_computation.4 | convolution fusion | flops 3224371200 | bytes 13107200 | tf_op jit(solution)/shard_map/dot_general | solution.py:59
  215.3 6.0 %copy.51 = bf16[8,64,6144]{2,0,1:T(8,128)(2,1)} copy(bf16[8,64,6144]{2,1,0:T(8,128)(2,1)S(1)} %convolution_convert_fusion.1) | data formatting | bytes 12582912 | tf_op jit(solution)/shard_map/convert_element_type | solution.py:63
  221.4 0.0 copy-start.4
  221.4 0.0 reduce-scatter.3.cloned.1.call-update
  221.4 0.3 all-gather.5.cloned.1.call-start
  221.6 67.2 %reduce-scatter.5.cloned.1.call-done = bf16[8,4,6144]{2,0,1:T(8,128)(2,1)} async-done(((bf16[8,64,6144]{2,0,1:T(8,128)(2,1)}), bf16[8,4,6144]{2,0,1:T(8,128)(2,1)}) %reduce-scatter.5.cloned.1.call-update) | async-done | bytes 393232 | tf_op jit(solution)/shard_map/reduce_scatter | solution.py:70
  288.9 1.3 copy.58
  290.2 14.1 %all_to_all.20 = bf16[8,4,6144]{2,1,0:T(4,128)(2,1)S(1)} all-to-all(bf16[8,4,6144]{2,1,0:T(4,128)(2,1)S(1)} %copy.58), channel_id=1, replica_groups=mesh['expert'=8,'shard'=16] {'expert'}, dimensions={0} | all-to-all | bytes 786432 | tf_op jit(solution)/shard_map/all_to_all | solution.py:73
  304.3 1.0 copy.59
  305.2 0.0 all-gather.5.cloned.1.call-update
  305.2 0.0 all-gather.3.cloned.1.call-start
  305.3 67.7 %reduce-scatter.3.cloned.1.call-done = bf16[8,4,6144]{2,0,1:T(8,128)(2,1)} async-done(((bf16[8,64,6144]{2,0,1:T(8,128)(2,1)}), bf16[8,4,6144]{2,0,1:T(8,128)(2,1)}) %reduce-scatter.3.cloned.1.call-update) | async-done | bytes 393232 | tf_op jit(solution)/shard_map/reduce_scatter | solution.py:62
  373.0 1.3 copy.52
  374.3 14.1 %all_to_all.21 = bf16[8,4,6144]{2,1,0:T(4,128)(2,1)S(1)} all-to-all(bf16[8,4,6144]{2,1,0:T(4,128)(2,1)S(1)} %copy.52), channel_id=1, replica_groups=mesh['expert'=8,'shard'=16] {'expert'}, dimensions={0} | all-to-all | bytes 786432 | tf_op jit(solution)/shard_map/all_to_all | solution.py:65
  388.3 1.0 copy.53
  389.3 0.0 all-gather.3.cloned.1.call-update
  389.3 0.1 mul.87
  389.5 0.0 copy-done.4
  389.5 47.9 %all-gather.5.cloned.1.call-done = bf16[8,64,6144]{2,0,1:T(8,128)(2,1)} async-done(((bf16[8,4,6144]{2,0,1:T(8,128)(2,1)}), bf16[8,64,6144]{2,0,1:T(8,128)(2,1)}) %all-gather.5.cloned.1.call-update) | async-done | bytes 6291472 | tf_op jit(solution)/shard_map/all_gather | solution.py:74
  437.4 8.8 %copy.60 = bf16[8,64,6144]{2,1,0:T(8,128)(2,1)} copy(bf16[8,64,6144]{2,0,1:T(8,128)(2,1)} %all-gather.5.cloned.1.call-done) | data formatting | bytes 12582912 | tf_op jit(solution)/shard_map/all_gather | solution.py:74
  446.2 10.7 %gather_fusion.1 = bf16[256,6144]{1,0:T(8,128)(2,1)} fusion(bf16[512,6144]{1,0:T(8,128)(2,1)} %bitcast.77, s32[1024]{0:T(1024)S(1)} %pad_clamp_fusion), kind=kCustom, calls=%fused_computation.1 | custom fusion | bytes 6292480 | tf_op jit(solution)/shard_map/gather | solution.py:21
  456.9 8.0 %reshape.104 = f32[128,2,6144]{2,1,0:T(2,128)} reshape(bf16[256,6144]{1,0:T(8,128)(2,1)} %gather_fusion.1) | data formatting | bytes 9437184 | tf_op jit(solution)/shard_map/convert_element_type | solution.py:21
  465.0 36.0 %all-gather.3.cloned.1.call-done = bf16[8,64,6144]{2,0,1:T(8,128)(2,1)} async-done(((bf16[8,4,6144]{2,0,1:T(8,128)(2,1)}), bf16[8,64,6144]{2,0,1:T(8,128)(2,1)}) %all-gather.3.cloned.1.call-update) | async-done | bytes 6291472 | tf_op jit(solution)/shard_map/all_gather | solution.py:66
  500.9 8.8 %copy.54 = bf16[8,64,6144]{2,1,0:T(8,128)(2,1)} copy(bf16[8,64,6144]{2,0,1:T(8,128)(2,1)} %all-gather.3.cloned.1.call-done) | data formatting | bytes 12582912 | tf_op jit(solution)/shard_map/all_gather | solution.py:66
  509.7 10.7 %gather_fusion = bf16[256,6144]{1,0:T(8,128)(2,1)} fusion(bf16[512,6144]{1,0:T(8,128)(2,1)} %bitcast.76, s32[1024]{0:T(1024)S(1)} %pad_clamp_fusion), kind=kCustom, calls=%fused_computation | custom fusion | bytes 6292480 | tf_op jit(solution)/shard_map/gather | solution.py:21
  520.5 7.6 %reshape.103 = f32[128,2,6144]{2,1,0:T(2,128)} reshape(bf16[256,6144]{1,0:T(8,128)(2,1)} %gather_fusion) | data formatting | bytes 9437184 | tf_op jit(solution)/shard_map/convert_element_type | solution.py:21
  528.1 16.2 %fusion.27 = (f32[128,1,6144]{2,1,0:T(1,128)S(1)}, f32[128,1,6144]{2,1,0:T(1,128)S(1)}, f32[128,1,6144]{2,1,0:T(1,128)S(1)}, f32[128,1,6144]{2,1,0:T(1,128)S(1)}) fusion(f32[128,2,6144]{2,1,0:T(2,128)} %reshape.104, f32[128,2,6144]{2,1,0:T(2,128)} %reshape.103), kind=kLoop, calls=%fused_computation.51 | loop fusion | bytes 25165824 | tf_op jit(solution)/shard_map/slice | solution.py:22
  544.3 0.0 copy-start.1
  544.3 8.1 %fusion.12 = (bf16[128,6144]{1,0:T(8,128)(2,1)}, bf16[128,6144]{1,0:T(8,128)(2,1)}) fusion(f32[128,1,6144]{2,1,0:T(1,128)S(1)} %get-tuple-element.3, f32[128,1,6144]{2,1,0:T(1,128)S(1)} %get-tuple-element.2, f32[128]{0:T(128)S(1)} %get-tuple-element.11, f32[128]{0:T(128)S(1)} %get-tuple-element.10, f32[128,1,6144]{2,1,0:T(1,128)S(1)} %get-tuple-element.14, ...), kind=kLoop, calls=%fused_computation.19 | loop fusion | flops 6291456 | bytes 15729664 | tf_op jit(solution)/shard_map/convert_element_type | solution.py:23
  552.4 0.0 copy-done.1
  (7 shorter events, 0.1 us)
Async XLA Ops:
  7.2 2.5 copy-start
  14.0 7.0 %copy-start.2 = (bf16[128,6144]{1,0:T(8,128)(2,1)S(1)}, bf16[128,6144]{1,0:T(8,128)(2,1)}, u32[]{:S(2)}) copy-start(bf16[128,6144]{1,0:T(8,128)(2,1)} %param.10) | copy-start | bytes 4718596
  14.0 78.3 %all-to-all-start = ((bf16[8,64,6144]{2,1,0:T(8,128)(2,1)}), bf16[8,64,6144]{2,1,0:T(8,128)(2,1)}, u32[]{:S(2)}, u32[]{:S(2)}) async-start(bf16[8,64,6144]{2,1,0:T(8,128)(2,1)} %bitcast.79), calls=%async_computation | async-start | bytes 12582912 | tf_op jit(solution)/shard_map/all_to_all | solution.py:51
  92.3 76.9 %all-to-all-start.2 = ((bf16[8,64,6144]{2,1,0:T(8,128)(2,1)}), bf16[8,64,6144]{2,1,0:T(8,128)(2,1)}, u32[]{:S(2)}, u32[]{:S(2)}) async-start(bf16[8,64,6144]{2,1,0:T(8,128)(2,1)} %bitcast.78), calls=%async_computation.3 | async-start | bytes 12582912 | tf_op jit(solution)/shard_map/all_to_all | solution.py:52
  97.9 191.0 %reduce-scatter.5.cloned.1.call-start = ((), (), s32[]{:S(2)}) async-start(), calls=%async_computation.8 | async-start | bytes 6684672 | tf_op jit(solution)/shard_map/reduce_scatter | solution.py:70
  176.8 1.0 copy-start.3
  208.8 164.1 %reduce-scatter.3.cloned.1.call-start = ((), (), s32[]{:S(2)}) async-start(), calls=%async_computation.6 | async-start | bytes 6684672 | tf_op jit(solution)/shard_map/reduce_scatter | solution.py:62
  221.4 168.1 %copy-start.4 = (f32[128,2]{0,1:T(2,128)S(1)}, f32[128,2]{0,1:T(2,128)}, u32[]{:S(2)}) copy-start(f32[128,2]{0,1:T(2,128)} %param.9) | copy-start | bytes 3076
  221.4 216.0 %all-gather.5.cloned.1.call-start = ((), (), s32[]{:S(2)}) async-start(), calls=%async_computation.9 | async-start | bytes 6684672 | tf_op jit(solution)/shard_map/all_gather | solution.py:74
  305.2 195.7 %all-gather.3.cloned.1.call-start = ((), (), s32[]{:S(2)}) async-start(), calls=%async_computation.7 | async-start | bytes 6684672 | tf_op jit(solution)/shard_map/all_gather | solution.py:66
  544.3 8.1 %copy-start.1 = (bf16[128,6144]{1,0:T(8,128)(2,1)S(1)}, bf16[128,6144]{1,0:T(8,128)(2,1)}, u32[]{:S(2)}) copy-start(bf16[128,6144]{1,0:T(8,128)(2,1)} %param.7) | copy-start | bytes 4718596
Sparse Core Ops, SparseCore 0:
  208.9 79.8 reduce-scatter.4
  292.3 80.6 reduce-scatter.2
  375.7 61.6 all-gather.4
  440.0 60.9 all-gather.2
where the time goes:
time: 568 us; the launch traced here: 559 us
  waiting for transfers between devices  341 us (60%)
  local copies, waits for them, and re-layouts  93.1 us (16%)
  matrix products  60.5 us (11%)
  blocking collectives  28.2 us (5%)
  between operations  14.1 us (2%)
  starting transfers between devices  12.8 us (2%)
  other arithmetic  8.93 us (2%)
    reduce_scatter x1, waiting for transfers between devices, per_device(): lax.psum_scatter(out_part.astype(jnp.bfloat16), 'shard', scatter_dimensio...  67.7 us
    reduce_scatter x1, waiting for transfers between devices, per_device(): lax.psum_scatter(grad_part.astype(jnp.bfloat16), 'shard', scatter_dimensi...  67.2 us
    all_to_all x1, waiting for transfers between devices, per_device(): lax.all_to_all(send_rows, 'expert', split_axis=0, concat_axis=0, tiled=True)  67 us
    all_to_all x1, waiting for transfers between devices, per_device(): lax.all_to_all(send_grad, 'expert', split_axis=0, concat_axis=0, tiled=True)  55.8 us
    all_gather x1, waiting for transfers between devices, per_device(): grad_back = lax.all_gather(grad_home, 'shard', axis=1, tiled=True)  47.9 us
    all_gather x1, waiting for transfers between devices, per_device(): out_back = lax.all_gather(out_home, 'shard', axis=1, tiled=True)  36 us
    gather x2, local copies, waits for them, and re-layouts, weighted_pair(): flat_rows[target].reshape(count_rows, 2, model_width).astype(jnp.float32)  21.4 us
    slice x1, local copies, waits for them, and re-layouts, weighted_pair(): chosen[:, 0, :]  16.2 us
  transfers between devices with their start and end apart: 6, of which 6 were waited for; matrix products, arithmetic and copies ran while one was open for 12% of the time, Pallas kernels for 0%

commit v1 on v0

--- a/solution.py
+++ b/solution.py
@@ -2,6 +2,13 @@
 import jax.numpy as jnp
 from jax import lax
 from jax.sharding import PartitionSpec as P
+
+
+def gather_over(x, mesh_axis, along):
+    size = lax.axis_size(mesh_axis)
+    tiles = jnp.stack([x for _ in range(size)])
+    tiles = lax.all_to_all(tiles, mesh_axis, split_axis=0, concat_axis=0)
+    return jnp.concatenate(tiles, axis=along)
 
 
 def backward_terms(rows_g, gate_act, up_act, w_gate, w_up, w_down):
@@ -71,7 +78,7 @@
         grad_part.astype(jnp.bfloat16), "shard", scatter_dimension=1, tiled=True
     )
     grad_home = lax.all_to_all(grad_sum, "expert", split_axis=0, concat_axis=0, tiled=True)
-    grad_back = lax.all_gather(grad_home, "shard", axis=1, tiled=True)
+    grad_back = gather_over(grad_home, "shard", 1)
     moe_out = weighted_pair(out_back, target, route_weights, count_rows, model_width)
     input_grad = weighted_pair(grad_back, target, route_weights, count_rows, model_width)
     return (moe_out, input_grad)

time: 568 us -> 539 us (0.949)
  waiting for transfers between devices: 341 us -> 172 us
  blocking collectives: 28.2 us -> 181 us
  matrix products: 60.5 us -> 40.9 us
  local copies, waits for them, and re-layouts: 93.1 us -> 110 us
  starting transfers between devices: 12.8 us -> 4.92 us
    all_to_all x0 -> x2, blocking collectives: none -> 156 us  [the longest x1 79.1 us: per_device(): lax.all_to_all(send_rows, 'expert', split_axis=0, concat_axis=0, tiled=True)]
    reduce_scatter x1, waiting for transfers between devices: 67.7 us -> 0.02 us  [per_device(): lax.psum_scatter(out_part.astype(jnp.bfloat16), 'shard', scatter_dimensio...]
    all_gather x1 -> x0, waiting for transfers between devices: 47.9 us -> none  [per_device(): grad_back = lax.all_gather(grad_home, 'shard', axis=1, tiled=True)]
    all_gather x1, waiting for transfers between devices: 36 us -> 0.02 us  [per_device(): out_back = lax.all_gather(out_home, 'shard', axis=1, tiled=True)]
    all_to_all x2 -> x1, waiting for transfers between devices: 123 us -> 106 us  [gather_over(): tiles = lax.all_to_all(tiles, mesh_axis, split_axis=0, concat_axis=0)]
    another operation x1 -> x3, local copies, waits for them, and re-layouts: 0.01 us -> 16.2 us  [the longest x1 10.4 us: weighted_pair(): flat_rows = returned.reshape(-1, model_width)]
    reshape x0 -> x1, local copies, waits for them, and re-layouts: none -> 9.41 us  [gather_over(): return jnp.concatenate(tiles, axis=along)]
    all_gather x1 -> x0, local copies, waits for them, and re-layouts: 8.82 us -> none  [per_device(): grad_back = lax.all_gather(grad_home, 'shard', axis=1, tiled=True)]
  transfers between devices with their start and end apart: 6 -> 4, of which waited for: 6 -> 2; matrix products, arithmetic and copies ran while one was open for 12% -> 15% of each run, Pallas kernels for 0% -> 0%
where the time goes in v1:
time: 539 us; the launch traced here: 533 us
  blocking collectives  181 us (34%)
  waiting for transfers between devices  172 us (32%)
  local copies, waits for them, and re-layouts  110 us (20%)
  matrix products  40.9 us (8%)
  between operations  14.4 us (3%)
  other arithmetic  8.94 us (2%)
    all_to_all x1, waiting for transfers between devices, gather_over(): tiles = lax.all_to_all(tiles, mesh_axis, split_axis=0, concat_axis=0)  106 us
    all_to_all x1, blocking collectives, per_device(): lax.all_to_all(send_rows, 'expert', split_axis=0, concat_axis=0, tiled=True)  79.1 us
    all_to_all x1, blocking collectives, per_device(): lax.all_to_all(send_grad, 'expert', split_axis=0, concat_axis=0, tiled=True)  76.5 us
    reduce_scatter x1, waiting for transfers between devices, per_device(): lax.psum_scatter(grad_part.astype(jnp.bfloat16), 'shard', scatter_dimensi...  66 us
    gather x2, local copies, waits for them, and re-layouts, weighted_pair(): flat_rows[target].reshape(count_rows, 2, model_width).astype(jnp.float32)  21.5 us
    slice x1, local copies, waits for them, and re-layouts, weighted_pair(): chosen[:, 0, :]  16.2 us
    convert_element_type x2, local copies, waits for them, and re-layouts, weighted_pair(): flat_rows[target].reshape(count_rows, 2, model_width).astype(jnp.float32)  15.5 us
    all_to_all x1, blocking collectives, per_device(): lax.all_to_all(grad_sum, 'expert', split_axis=0, concat_axis=0, tiled=True)  14.1 us
  transfers between devices with their start and end apart: 4, of which 2 were waited for; matrix products, arithmetic and copies ran while one was open for 15% of the time, Pallas kernels for 0%

profile of v1, /device:TPU:1, one launch (start us, length us, event | category | flops | bytes accessed | tf_op | source)
XLA Modules:
  0.0 533.0 jit_solution(17366004538209256132)
XLA Ops:
  7.2 0.0 copy-start
  7.2 0.0 reduce-scatter.3.cloned.1.call-start
  7.2 0.9 copy.47
  8.1 0.1 eq.44
  8.3 0.1 eq.40
  8.4 0.6 reduce-window.6
  9.0 0.2 slice_reduce_fusion
  9.3 0.1 fusion.22
  9.4 0.1 reduce_sum.14
  9.5 0.1 copy.50
  9.6 0.1 fusion.20
  9.7 0.0 copy-done
  9.7 0.0 slice-start
  9.7 1.8 convolution_convert_fusion.2
  11.5 0.0 slice-start.1
  11.5 79.1 %all_to_all.25 = bf16[8,64,6144]{2,1,0:T(8,128)(2,1)S(1)} all-to-all(bf16[8,64,6144]{2,1,0:T(8,128)(2,1)S(1)} %bitcast.78), channel_id=1, replica_groups=mesh['expert'=8,'shard'=16] {'expert'}, dimensions={0} | all-to-all | bytes 12582912 | tf_op jit(solution)/shard_map/all_to_all | solution.py:58
  90.6 0.0 slice-done
  90.6 0.0 slice-done.1
  90.6 3.4 fusion.8
  94.0 0.0 slice-start.5
  94.0 7.4 %multiply_convert_fusion.2 = (bf16[512,512]{1,0:T(8,128)(2,1)S(1)}, f32[512,512]{1,0:T(8,128)}) fusion(f32[512,512]{1,0:T(8,128)S(1)} %fusion.8, bf16[512,6144]{1,0:T(8,128)(2,1)S(1)} %bitcast.80, bf16[1,6144,512]{2,1,0:T(8,128)(2,1)} %param.12), kind=kOutput, calls=%fused_computation.30 | convolution fusion | flops 3222798336 | bytes 15204352 | tf_op jit(solution)/shard_map/dot_general | solution.py:64
  101.4 0.0 slice-done.4
  101.4 3.6 convolution_convert_fusion.1
  105.0 6.0 %copy.51 = bf16[8,64,6144]{2,0,1:T(8,128)(2,1)} copy(bf16[8,64,6144]{2,1,0:T(8,128)(2,1)S(1)} %convolution_convert_fusion.1) | data formatting | bytes 12582912 | tf_op jit(solution)/shard_map/convert_element_type | solution.py:70
  111.1 0.0 reduce-scatter.3.cloned.1.call-update
  111.1 0.0 reduce-scatter.5.cloned.1.call-start
  111.1 1.3 copy-done.2
  112.5 1.8 convolution_convert_fusion
  114.3 0.0 slice-start.7
  114.3 0.0 slice-start.2
  114.3 76.5 %all_to_all.26 = bf16[8,64,6144]{2,1,0:T(8,128)(2,1)S(1)} all-to-all(bf16[8,64,6144]{2,1,0:T(8,128)(2,1)S(1)} %bitcast.77), channel_id=1, replica_groups=mesh['expert'=8,'shard'=16] {'expert'}, dimensions={0} | all-to-all | bytes 12582912 | tf_op jit(solution)/shard_map/all_to_all | solution.py:59
  190.8 0.0 copy-start.3
  190.8 3.4 fusion.1
  194.3 0.0 copy-start.4
  194.3 1.0 copy-done.4
  195.3 0.0 slice-done.2
  195.3 6.7 %fusion.6 = f32[512,6144]{1,0:T(8,128)} fusion(bf16[1,6144,512]{2,1,0:T(8,128)(2,1)S(1)} %bitcast.86, f32[512,512]{1,0:T(8,128)S(1)} %fusion.8, f32[512,512]{1,0:T(8,128)S(1)} %fusion.1, f32[512,512]{1,0:T(8,128)S(1)} %copy-done.3), kind=kOutput, calls=%fused_computation.12 | convolution fusion | flops 3223846912 | bytes 22020096 | tf_op jit(solution)/shard_map/dot_general | solution.py:22
  202.0 12.8 %add_convert_fusion = bf16[512,6144]{1,0:T(8,128)(2,1)} fusion(f32[512,6144]{1,0:T(8,128)} %fusion.6, bf16[1,6144,512]{2,1,0:T(8,128)(2,1)} %param.12, f32[512,512]{1,0:T(8,128)} %copy-done.4, f32[512,512]{1,0:T(8,128)S(1)} %fusion.8), kind=kOutput, calls=%fused_computation.2 | convolution fusion | flops 3229089792 | bytes 27262976 | tf_op jit(solution)/shard_map/dot_general | solution.py:23
  214.8 8.9 %copy.57 = bf16[8,64,6144]{2,0,1:T(8,128)(2,1)} copy(bf16[8,64,6144]{2,1,0:T(8,128)(2,1)} %bitcast.81) | data formatting | bytes 12582912 | tf_op jit(solution)/shard_map/convert_element_type | solution.py:78
  223.6 0.0 reduce-scatter.5.cloned.1.call-update
  223.6 0.0 all-gather.2.cloned.1.call-start
  223.7 0.0 reduce-scatter.3.cloned.1.call-done
  223.7 1.3 copy.52
  225.0 11.7 %all_to_all.27 = bf16[8,4,6144]{2,1,0:T(4,128)(2,1)S(1)} all-to-all(bf16[8,4,6144]{2,1,0:T(4,128)(2,1)S(1)} %copy.52), channel_id=1, replica_groups=mesh['expert'=8,'shard'=16] {'expert'}, dimensions={0} | all-to-all | bytes 786432 | tf_op jit(solution)/shard_map/all_to_all | solution.py:72
  236.7 1.0 copy.53
  237.7 0.0 all-gather.2.cloned.1.call-update
  237.7 66.0 %reduce-scatter.5.cloned.1.call-done = bf16[8,4,6144]{2,0,1:T(8,128)(2,1)} async-done(((bf16[8,64,6144]{2,0,1:T(8,128)(2,1)}), bf16[8,4,6144]{2,0,1:T(8,128)(2,1)}) %reduce-scatter.5.cloned.1.call-update) | async-done | bytes 393232 | tf_op jit(solution)/shard_map/reduce_scatter | solution.py:77
  303.7 1.3 copy.58
  305.0 14.1 %all_to_all.28 = bf16[8,4,6144]{2,1,0:T(4,128)(2,1)S(1)} all-to-all(bf16[8,4,6144]{2,1,0:T(4,128)(2,1)S(1)} %copy.58), channel_id=1, replica_groups=mesh['expert'=8,'shard'=16] {'expert'}, dimensions={0} | all-to-all | bytes 786432 | tf_op jit(solution)/shard_map/all_to_all | solution.py:80
  319.1 5.7 %stack.2 = bf16[16,8,4,6144]{3,2,1,0:T(4,128)(2,1)} broadcast(bf16[8,4,6144]{2,1,0:T(4,128)(2,1)S(1)} %all_to_all.28), dimensions={1,2,3} | broadcast | bytes 6684672 | tf_op jit(solution)/shard_map/stack | solution.py:9
  324.8 4.8 all-to-all-start.4
  329.6 0.1 mul.87
  329.8 106.2 %all-to-all-done.4 = bf16[16,8,4,6144]{3,2,1,0:T(4,128)(2,1)} async-done(((bf16[16,8,4,6144]{3,2,1,0:T(4,128)(2,1)}), bf16[16,8,4,6144]{3,2,1,0:T(4,128)(2,1)}, u32[]{:S(2)}, u32[]{:S(2)}) %all-to-all-start.4) | async-done | bytes 6291488 | tf_op jit(solution)/shard_map/all_to_all | solution.py:10
  436.0 9.4 %copy.59 = bf16[8,16,4,6144]{3,2,1,0:T(4,128)(2,1)} copy(bf16[8,16,4,6144]{3,2,0,1:T(4,128)(2,1)} %bitcast.19) | data formatting | bytes 12582912 | tf_op jit(solution)/shard_map/reshape | solution.py:11
  445.4 10.4 %reshape_reshape.3 = bf16[512,6144]{1,0:T(8,128)(2,1)} reshape(bf16[8,16,4,6144]{3,2,1,0:T(4,128)(2,1)} %copy.59) | data formatting | bytes 12582912 | tf_op jit(solution)/shard_map/reshape;reshape | solution.py:27
  455.8 10.7 %gather_fusion.1 = bf16[256,6144]{1,0:T(8,128)(2,1)} fusion(bf16[512,6144]{1,0:T(8,128)(2,1)} %reshape_reshape.3, s32[1024]{0:T(1024)S(1)} %pad_clamp_fusion), kind=kCustom, calls=%fused_computation.1 | custom fusion | bytes 6292480 | tf_op jit(solution)/shard_map/gather | solution.py:28
  466.6 7.8 %reshape.106 = f32[128,2,6144]{2,1,0:T(2,128)} reshape(bf16[256,6144]{1,0:T(8,128)(2,1)} %gather_fusion.1) | data formatting | bytes 9437184 | tf_op jit(solution)/shard_map/convert_element_type | solution.py:28
  474.4 0.0 all-gather.2.cloned.1.call-done
  474.4 8.8 %copy.54 = bf16[8,64,6144]{2,1,0:T(8,128)(2,1)} copy(bf16[8,64,6144]{2,0,1:T(8,128)(2,1)} %all-gather.2.cloned.1.call-done) | data formatting | bytes 12582912 | tf_op jit(solution)/shard_map/all_gather | solution.py:73
  483.3 10.7 %gather_fusion = bf16[256,6144]{1,0:T(8,128)(2,1)} fusion(bf16[512,6144]{1,0:T(8,128)(2,1)} %bitcast.76, s32[1024]{0:T(1024)S(1)} %pad_clamp_fusion), kind=kCustom, calls=%fused_computation | custom fusion | bytes 6292480 | tf_op jit(solution)/shard_map/gather | solution.py:28
  494.0 7.7 %reshape.105 = f32[128,2,6144]{2,1,0:T(2,128)} reshape(bf16[256,6144]{1,0:T(8,128)(2,1)} %gather_fusion) | data formatting | bytes 9437184 | tf_op jit(solution)/shard_map/convert_element_type | solution.py:28
  501.7 16.2 %fusion.27 = (f32[128,1,6144]{2,1,0:T(1,128)S(1)}, f32[128,1,6144]{2,1,0:T(1,128)S(1)}, f32[128,1,6144]{2,1,0:T(1,128)S(1)}, f32[128,1,6144]{2,1,0:T(1,128)S(1)}) fusion(f32[128,2,6144]{2,1,0:T(2,128)} %reshape.106, f32[128,2,6144]{2,1,0:T(2,128)} %reshape.105), kind=kLoop, calls=%fused_computation.51 | loop fusion | bytes 25165824 | tf_op jit(solution)/shard_map/slice | solution.py:29
  517.9 0.0 copy-start.1
  517.9 8.1 %fusion.12 = (bf16[128,6144]{1,0:T(8,128)(2,1)}, bf16[128,6144]{1,0:T(8,128)(2,1)}) fusion(f32[128,1,6144]{2,1,0:T(1,128)S(1)} %get-tuple-element.3, f32[128,1,6144]{2,1,0:T(1,128)S(1)} %get-tuple-element.2, f32[128]{0:T(128)S(1)} %get-tuple-element.11, f32[128]{0:T(128)S(1)} %get-tuple-element.10, f32[128,1,6144]{2,1,0:T(1,128)S(1)} %get-tuple-element.14, ...), kind=kLoop, calls=%fused_computation.19 | loop fusion | flops 6291456 | bytes 15729664 | tf_op jit(solution)/shard_map/convert_element_type | solution.py:30
  (23 shorter events, 0.1 us)
Async XLA Ops:
  7.2 2.5 copy-start
  7.2 216.5 %reduce-scatter.3.cloned.1.call-start = ((), (), s32[]{:S(2)}) async-start(), calls=%async_computation.7 | async-start | bytes 6684672 | tf_op jit(solution)/shard_map/reduce_scatter | solution.py:69
  9.7 80.9 %slice-start = ((s8[6291456]{0:T(1024)(128)(4,1)}), s8[4194304]{0:T(1024)(128)(4,1)S(1)}, s32[]{:S(2)}) async-start(s8[6291456]{0:T(1024)(128)(4,1)} %bitcast.83), calls=%async_computation.10 | async-start | bytes 8388608
  11.5 79.1 %slice-start.1 = ((s8[6291456]{0:T(1024)(128)(4,1)}), s8[2097152]{0:T(1024)(128)(4,1)S(1)}, s32[]{:S(2)}) async-start(s8[6291456]{0:T(1024)(128)(4,1)} %bitcast.83), calls=%async_computation.11 | async-start | bytes 4194304
  90.6 10.8 %slice-start.4 = ((s8[6291456]{0:T(1024)(128)(4,1)}), s8[4194304]{0:T(1024)(128)(4,1)S(1)}, s32[]{:S(2)}) async-start(s8[6291456]{0:T(1024)(128)(4,1)} %bitcast.89), calls=%async_computation.14 | async-start | bytes 8388608
  94.0 7.4 %slice-start.5 = ((s8[6291456]{0:T(1024)(128)(4,1)}), s8[2097152]{0:T(1024)(128)(4,1)S(1)}, s32[]{:S(2)}) async-start(s8[6291456]{0:T(1024)(128)(4,1)} %bitcast.89), calls=%async_computation.15 | async-start | bytes 4194304
  111.1 1.4 copy-start.2
  111.1 192.6 %reduce-scatter.5.cloned.1.call-start = ((), (), s32[]{:S(2)}) async-start(), calls=%async_computation.9 | async-start | bytes 6684672 | tf_op jit(solution)/shard_map/reduce_scatter | solution.py:77
  112.5 78.3 %slice-start.6 = ((s8[6291456]{0:T(1024)(128)(4,1)}), s8[4194304]{0:T(1024)(128)(4,1)S(1)}, s32[]{:S(2)}) async-start(s8[6291456]{0:T(1024)(128)(4,1)} %bitcast.91), calls=%async_computation.16 | async-start | bytes 8388608
  114.3 76.6 %slice-start.7 = ((s8[6291456]{0:T(1024)(128)(4,1)}), s8[2097152]{0:T(1024)(128)(4,1)S(1)}, s32[]{:S(2)}) async-start(s8[6291456]{0:T(1024)(128)(4,1)} %bitcast.91), calls=%async_computation.17 | async-start | bytes 4194304
  114.3 81.0 %slice-start.2 = ((s8[6291456]{0:T(1024)(128)(4,1)}), s8[4194304]{0:T(1024)(128)(4,1)S(1)}, s32[]{:S(2)}) async-start(s8[6291456]{0:T(1024)(128)(4,1)} %bitcast.85), calls=%async_computation.12 | async-start | bytes 8388608
  190.8 4.4 slice-start.3
  190.8 4.4 copy-start.3
  194.3 1.0 copy-start.4
  223.6 250.8 %all-gather.2.cloned.1.call-start = ((), (), s32[]{:S(2)}) async-start(), calls=%async_computation.8 | async-start | bytes 6684672 | tf_op jit(solution)/shard_map/all_gather | solution.py:73
  324.8 5.0 copy-start.5
  324.8 111.2 %all-to-all-start.4 = ((bf16[16,8,4,6144]{3,2,1,0:T(4,128)(2,1)}), bf16[16,8,4,6144]{3,2,1,0:T(4,128)(2,1)}, u32[]{:S(2)}, u32[]{:S(2)}) async-start(bf16[16,8,4,6144]{3,2,1,0:T(4,128)(2,1)} %stack.2), calls=%async_computation.6 | async-start | bytes 12582912 | tf_op jit(solution)/shard_map/all_to_all | solution.py:10
  517.9 8.1 %copy-start.1 = (bf16[128,6144]{1,0:T(8,128)(2,1)S(1)}, bf16[128,6144]{1,0:T(8,128)(2,1)}, u32[]{:S(2)}) copy-start(bf16[128,6144]{1,0:T(8,128)(2,1)} %param.7) | copy-start | bytes 4718596
Sparse Core Ops, SparseCore 0:
  111.2 79.9 reduce-scatter.2
  223.8 79.8 reduce-scatter.4
  306.4 130.3 all-gather.1
